TPU v7x, 32 devices: a whole 2x2x4 slice. The times are simulated.
32 devices in a mesh: seq: 2 (over x), batch: 16 (over z, y, core).
Axes of the slice: x: 2, y: 2, z: 4, core: 2. Of those that a mesh axis runs over, the one named last changes fastest.
Arguments:
- inputs: bfloat16 [16, 1024, 768], P('batch', 'seq'), may hold values from -6 to 6
- cotangent: bfloat16 [16, 1024, 768], P('batch', 'seq'), may hold values from -6 to 6
- cond_mask: int32 [16], P('batch'), may hold values 0 or 1
- timestep: int32 [16], P('batch'), may hold values from 0 to 999
- embed_table: float32 [1000, 768], replicated, may hold values from -6 to 6
- mix_weight: bfloat16 [768, 2304], replicated, may hold values from -0.21875 to 0.21875
- project_weight: bfloat16 [768, 768], replicated, may hold values from -3 to 3
- up_weight: bfloat16 [768, 3072], replicated, may hold values from -0.21875 to 0.21875
- down_weight: bfloat16 [3072, 768], replicated, may hold values from -0.109375 to 0.109375
- cond_weight: bfloat16 [768, 4608], replicated, may hold values from -0.21875 to 0.21875
- cond_bias: float32 [4608], replicated, may hold values from -3 to 3
Outputs:
- layer_output: bfloat16 [16, 1024, 768], P('batch', 'seq')
- input_grad: float32 [16, 1024, 768], P('batch', 'seq')
- grad_mix: float32 [768, 2304], P('batch')
- grad_project: float32 [768, 768], P('batch')
- grad_up: float32 [768, 3072], P('batch')
- grad_down: float32 [3072, 768], P('batch')
- grad_cond: float32 [768, 4608], P('batch')
- grad_bias: float32 [4608], P('batch')
All inputs are finite; a program needn't handle non-finite values. No bound on the sum of `cond_mask` on one device may be relied on, other than what follows from the above.
Results may differ from a plain program's by a relative error of at most 0.01.
The roundings to bfloat16 on the way count: a program that leaves them out, or rounds other values in their place, can miss the bound.
Values may be sent and summed in bfloat16 or wider, within the bound.
A program may use at most 256 MiB of HBM per device.

v0:
```python
import jax
import jax.numpy as jnp
from jax import lax
from jax.sharding import PartitionSpec as P

HEAD = 64


eps_norm = 1e-06
theta_base = 10000.0
highest = lax.Precision.HIGHEST


def normalize(values):
    row_mean = jnp.mean(values, axis=-1, keepdims=True)
    centered = values - row_mean
    row_var = jnp.mean(centered * centered, axis=-1, keepdims=True)
    inverse = lax.rsqrt(row_var + eps_norm)
    return (centered * inverse, inverse)


def norm_back(grad_normed, normed, inverse):
    grad_mean = jnp.mean(grad_normed, axis=-1, keepdims=True)
    cross_mean = jnp.mean(grad_normed * normed, axis=-1, keepdims=True)
    return inverse * (grad_normed - grad_mean - normed * cross_mean)


def rotary_tables(count, offset, head_size):
    half_size = head_size // 2
    freqs = theta_base ** (-jnp.arange(half_size, dtype=jnp.float32) * 2.0 / head_size)
    places = (offset + jnp.arange(count, dtype=jnp.int32)).astype(jnp.float32)
    angles = places[:, None] * freqs[None, :]
    return (jnp.cos(angles)[:, None, :], jnp.sin(angles)[:, None, :])


def rotate(values, cosine_table, sine_table):
    half_size = values.shape[-1] // 2
    first_half = values[..., :half_size]
    second = values[..., half_size:]
    return jnp.concatenate(
        [
            first_half * cosine_table - second * sine_table,
            second * cosine_table + first_half * sine_table,
        ],
        axis=-1,
    )


def unrotate(grads, cosine_table, sine_table):
    half_size = grads.shape[-1] // 2
    first_half = grads[..., :half_size]
    second = grads[..., half_size:]
    return jnp.concatenate(
        [
            first_half * cosine_table + second * sine_table,
            second * cosine_table - first_half * sine_table,
        ],
        axis=-1,
    )


def group_size(seq_count, pos_count):
    return min(seq_count, max(1, 512 // pos_count))


def grouped(values, size):
    return values.reshape((values.shape[0] // size, size) + values.shape[1:])


def flatten_groups(values):
    return values.reshape((values.shape[0] * values.shape[1],) + values.shape[2:])


def collect(key_part, value_part):
    return (
        lax.all_gather(key_part, "seq", axis=1, tiled=True),
        lax.all_gather(value_part, "seq", axis=1, tiled=True),
    )


def attend_forward(query, key_all, value_all):
    size = group_size(query.shape[0], query.shape[1])

    def one_group(items):
        query_rows, key_rows, value_rows = items
        scores = jnp.einsum(
            "sqhe,skhe->shqk", query_rows, key_rows, preferred_element_type=jnp.float32
        ) * HEAD ** (-0.5)
        probs = jax.nn.softmax(scores, axis=-1)
        return jnp.einsum(
            "shqk,skhe->sqhe",
            probs.astype(jnp.bfloat16),
            value_rows,
            preferred_element_type=jnp.float32,
        ).astype(jnp.bfloat16)

    return flatten_groups(
        lax.map(one_group, (grouped(query, size), grouped(key_all, size), grouped(value_all, size)))
    )


def layer_forward(xin, pieces, weights, cosine_table, sine_table):
    shift_mix, scale_mix, gate_mix, shift_feed, scale_feed, gate_feed = pieces
    mix_weight, project_weight, up_weight, down_weight = weights
    seq_count, pos_count, model_width = xin.shape
    head_count = model_width // HEAD
    row_count = seq_count * pos_count
    norm_mix, inverse_mix = normalize(xin)
    a_in = (norm_mix * (1.0 + scale_mix) + shift_mix).astype(jnp.bfloat16)
    projected = jnp.dot(
        a_in.reshape(row_count, model_width), mix_weight, preferred_element_type=jnp.float32
    )
    projected = projected.reshape(seq_count, pos_count, 3, head_count, HEAD)
    query = rotate(projected[:, :, 0], cosine_table, sine_table).astype(jnp.bfloat16)
    key_part = rotate(projected[:, :, 1], cosine_table, sine_table).astype(jnp.bfloat16)
    value_part = projected[:, :, 2].astype(jnp.bfloat16)
    key_all, value_all = collect(key_part, value_part)
    mixed = attend_forward(query, key_all, value_all)
    mixed_rows = mixed.reshape(row_count, model_width)
    branch_mix = jnp.dot(mixed_rows, project_weight, preferred_element_type=jnp.float32).reshape(
        seq_count, pos_count, model_width
    )
    middle = xin + gate_mix * branch_mix
    norm_feed, inverse_feed = normalize(middle)
    b_in = (norm_feed * (1.0 + scale_feed) + shift_feed).astype(jnp.bfloat16)
    b_rows = b_in.reshape(row_count, model_width)
    preact = jnp.dot(b_rows, up_weight, preferred_element_type=jnp.float32)
    hidden = jax.nn.gelu(preact).astype(jnp.bfloat16)
    branch_feed = jnp.dot(hidden, down_weight, preferred_element_type=jnp.float32).reshape(
        seq_count, pos_count, model_width
    )
    output = middle + gate_feed * branch_feed
    return {
        "output": output,
        "norm_mix": norm_mix,
        "inverse_mix": inverse_mix,
        "a_in": a_in,
        "query": query,
        "key_part": key_part,
        "value_part": value_part,
        "key_all": key_all,
        "value_all": value_all,
        "mixed_rows": mixed_rows,
        "branch_mix": branch_mix,
        "norm_feed": norm_feed,
        "inverse_feed": inverse_feed,
        "b_rows": b_rows,
        "preact": preact,
        "hidden": hidden,
        "branch_feed": branch_feed,
    }


def per_device(
    inputs,
    cotangent,
    cond_mask,
    timestep,
    embed_table,
    mix_weight,
    project_weight,
    up_weight,
    down_weight,
    cond_weight,
    cond_bias,
):
    seq_count, pos_count, model_width = inputs.shape
    head_count = model_width // HEAD
    row_count = seq_count * pos_count
    score_scale = HEAD ** (-0.5)
    size = group_size(seq_count, pos_count)
    cosine_table, sine_table = rotary_tables(pos_count, lax.axis_index("seq") * pos_count, HEAD)
    cond_code = jax.nn.silu(embed_table[timestep]).astype(jnp.bfloat16)
    modulation = jnp.dot(cond_code, cond_weight, preferred_element_type=jnp.float32) + cond_bias
    pieces = [
        modulation[:, slot_index * model_width : (slot_index + 1) * model_width][:, None, :]
        for slot_index in range(6)
    ]
    shift_mix, scale_mix, gate_mix, shift_feed, scale_feed, gate_feed = pieces
    weights = (mix_weight, project_weight, up_weight, down_weight)
    inputs_f32 = inputs.astype(jnp.float32)
    first_pass = layer_forward(inputs_f32, pieces, weights, cosine_table, sine_table)["output"]
    xin = inputs_f32 + cond_mask.astype(jnp.float32)[:, None, None] * first_pass
    saved = layer_forward(xin, pieces, weights, cosine_table, sine_table)
    layer_output = saved["output"].astype(jnp.bfloat16)
    grad_output = cotangent.astype(jnp.float32)
    grad_gate_feed = jnp.sum(grad_output * saved["branch_feed"], axis=1)
    grad_branch_feed = (
        (gate_feed * grad_output).astype(jnp.bfloat16).reshape(row_count, model_width)
    )
    grad_down = jnp.dot(saved["hidden"].T, grad_branch_feed, preferred_element_type=jnp.float32)
    grad_hidden = jnp.dot(grad_branch_feed, down_weight.T, preferred_element_type=jnp.float32)
    gelu_pull = jax.vjp(jax.nn.gelu, saved["preact"])[1]
    grad_preact = gelu_pull(grad_hidden)[0].astype(jnp.bfloat16)
    grad_up = jnp.dot(saved["b_rows"].T, grad_preact, preferred_element_type=jnp.float32)
    grad_b_in = jnp.dot(grad_preact, up_weight.T, preferred_element_type=jnp.float32).reshape(
        seq_count, pos_count, model_width
    )
    grad_shift_feed = jnp.sum(grad_b_in, axis=1)
    grad_scale_feed = jnp.sum(grad_b_in * saved["norm_feed"], axis=1)
    grad_middle = grad_output + norm_back(
        grad_b_in * (1.0 + scale_feed), saved["norm_feed"], saved["inverse_feed"]
    )
    grad_gate_mix = jnp.sum(grad_middle * saved["branch_mix"], axis=1)
    grad_branch_mix = (gate_mix * grad_middle).astype(jnp.bfloat16).reshape(row_count, model_width)
    grad_project = jnp.dot(
        saved["mixed_rows"].T, grad_branch_mix, preferred_element_type=jnp.float32
    )
    grad_mixed = jnp.dot(grad_branch_mix, project_weight.T, preferred_element_type=jnp.float32)
    grad_mixed = grad_mixed.reshape(seq_count, pos_count, head_count, HEAD).astype(jnp.bfloat16)
    key_all, value_all = (
        lax.all_gather(saved["key_part"], "seq", axis=1, tiled=True),
        lax.all_gather(saved["value_part"], "seq", axis=1, tiled=True),
    )
    query = saved["query"]

    def row_group(items):
        query_rows, grad_rows, key_rows, value_rows = items
        scores = (
            jnp.einsum("sqhe,skhe->shqk", query_rows, key_rows, preferred_element_type=jnp.float32)
            * score_scale
        )
        row_top = jax.nn.logsumexp(scores, axis=-1, keepdims=True)
        probs = jnp.exp(scores - row_top)
        grad_probs = jnp.einsum(
            "sqhe,skhe->shqk", grad_rows, value_rows, preferred_element_type=jnp.float32
        )
        row_delta = jnp.sum(probs * grad_probs, axis=-1, keepdims=True)
        grad_scores = (probs * (grad_probs - row_delta)).astype(jnp.bfloat16)
        grad_query_rows = (
            jnp.einsum("shqk,skhe->sqhe", grad_scores, key_rows, preferred_element_type=jnp.float32)
            * score_scale
        )
        grad_key_rows = (
            jnp.einsum(
                "shqk,sqhe->skhe", grad_scores, query_rows, preferred_element_type=jnp.float32
            )
            * score_scale
        )
        grad_value_rows = jnp.einsum(
            "shqk,sqhe->skhe",
            probs.astype(jnp.bfloat16),
            grad_rows,
            preferred_element_type=jnp.float32,
        )
        return (grad_query_rows, grad_key_rows, grad_value_rows)

    results = lax.map(
        row_group,
        (
            grouped(query, size),
            grouped(grad_mixed, size),
            grouped(key_all, size),
            grouped(value_all, size),
        ),
    )
    grad_query = flatten_groups(results[0])
    grad_key_all = flatten_groups(results[1])
    grad_value_all = flatten_groups(results[2])
    grad_key, grad_value = (
        lax.psum_scatter(grad_key_all, "seq", scatter_dimension=1, tiled=True),
        lax.psum_scatter(grad_value_all, "seq", scatter_dimension=1, tiled=True),
    )
    grad_projected = jnp.stack(
        [
            unrotate(grad_query, cosine_table, sine_table),
            unrotate(grad_key, cosine_table, sine_table),
            grad_value,
        ],
        axis=2,
    )
    grad_projected = grad_projected.reshape(row_count, 3 * model_width).astype(jnp.bfloat16)
    grad_mix = jnp.dot(
        saved["a_in"].reshape(row_count, model_width).T,
        grad_projected,
        preferred_element_type=jnp.float32,
    )
    grad_a_in = jnp.dot(grad_projected, mix_weight.T, preferred_element_type=jnp.float32).reshape(
        seq_count, pos_count, model_width
    )
    grad_shift_mix = jnp.sum(grad_a_in, axis=1)
    grad_scale_mix = jnp.sum(grad_a_in * saved["norm_mix"], axis=1)
    input_grad = grad_middle + norm_back(
        grad_a_in * (1.0 + scale_mix), saved["norm_mix"], saved["inverse_mix"]
    )
    grad_modulation = jnp.concatenate(
        [
            grad_shift_mix,
            grad_scale_mix,
            grad_gate_mix,
            grad_shift_feed,
            grad_scale_feed,
            grad_gate_feed,
        ],
        axis=-1,
    )
    grad_cond = jnp.dot(cond_code.astype(jnp.float32).T, grad_modulation, precision=highest)
    grad_bias = jnp.sum(grad_modulation, axis=0)
    all_shares = (
        lax.psum_scatter(grad_mix, "batch", scatter_dimension=0, tiled=True),
        lax.psum_scatter(grad_project, "batch", scatter_dimension=0, tiled=True),
        lax.psum_scatter(grad_up, "batch", scatter_dimension=0, tiled=True),
        lax.psum_scatter(grad_down, "batch", scatter_dimension=0, tiled=True),
        lax.psum_scatter(grad_cond, "batch", scatter_dimension=0, tiled=True),
        lax.psum_scatter(grad_bias, "batch", scatter_dimension=0, tiled=True),
    )
    all_shares = lax.psum(
        (all_shares[0], all_shares[1], all_shares[2], all_shares[3], all_shares[4], all_shares[5]),
        "seq",
    )
    share_mix, share_project, share_up, share_down, share_cond, share_bias = all_shares
    return (
        layer_output,
        input_grad,
        share_mix,
        share_project,
        share_up,
        share_down,
        share_cond,
        share_bias,
    )


def solution(mesh):
    placed = (
        P("batch", "seq", None),
        P("batch", "seq", None),
        P("batch"),
        P("batch"),
        P(),
        P(),
        P(),
        P(),
        P(),
        P(),
        P(),
    )
    return jax.shard_map(
        per_device,
        mesh=mesh,
        in_specs=placed,
        out_specs=(
            P("batch", "seq", None),
            P("batch", "seq", None),
            P("batch", None),
            P("batch", None),
            P("batch", None),
            P("batch", None),
            P("batch", None),
            P("batch"),
        ),
        check_vma=False,
    )
```

profile of v0, /device:TPU:0, one launch (start us, length us, event | category | flops | bytes accessed | tf_op | source)
XLA Modules:
  0.0 981.1 jit_solution(5992751511020466136)
XLA Ops:
  12.2 4.1 convolution_reduce_fusion
  16.9 5.8 copy.22
  22.8 4.3 convolution_bitcast_fusion.1
  27.5 1.6 copy-done.5
  31.2 2.4 slice.186
  34.3 26.9 %all-gather.7.cloned.1.call-done = bf16[1,1024,12,64]{1,3,2,0:T(8,128)(2,1)} async-done(((bf16[1,512,12,64]{1,3,2,0:T(8,128)(2,1)}), bf16[1,1024,12,64]{1,3,2,0:T(8,128)(2,1)}) %all-gather.7.cloned.1.call-update) | async-done | bytes 1572880 | tf_op jit(solution)/shard_map/all_gather | solution.py:76
  61.2 13.4 %fusion.140 = (f32[12,512]{1,0:T(8,128)S(1)}, f32[12,512,1024]{2,1,0:T(8,128)}) fusion(bf16[1,1024,12,64]{1,3,2,0:T(8,128)(2,1)} %all-gather.7.cloned.1.call-done, bf16[512,12,32]{0,2,1:T(8,128)(2,1)S(1)} %get-tuple-element.113, bf16[512,12,32]{0,2,1:T(8,128)(2,1)S(1)} %get-tuple-element.112), kind=kOutput, calls=%fused_computation.211 | convolution fusion | flops 825754624 | bytes 27549696 | tf_op jit(solution)/shard_map/while/body/eval_jaxpr/sub | solution.py:89
  74.6 15.9 %all-gather.11.cloned.1.call-done = bf16[1,1024,1,12,64]{1,4,3,2,0:T(8,128)(2,1)} async-done(((bf16[1,512,1,12,64]{1,4,3,2,0:T(8,128)(2,1)}), bf16[1,1024,1,12,64]{1,4,3,2,0:T(8,128)(2,1)}) %all-gather.11.cloned.1.call-update) | async-done | bytes 1572880 | tf_op jit(solution)/shard_map/all_gather | solution.py:77
  90.5 11.0 %fusion.72 = bf16[12,64,512]{2,1,0:T(8,128)(2,1)S(1)} fusion(f32[12,512,1024]{2,1,0:T(8,128)} %get-tuple-element.129, f32[12,512]{1,0:T(8,128)S(1)} %get-tuple-element.128, bf16[1,1024,1,12,64]{1,4,3,2,0:T(8,128)(2,1)} %all-gather.11.cloned.1.call-done), kind=kOutput, calls=%fused_computation.111 | convolution fusion | flops 818282496 | bytes 27549696 | tf_op jit(solution)/shard_map/while/body/eval_jaxpr/shqk,skhe->sqhe/dot_general | solution.py:90
  103.6 10.8 %fusion.146 = (f32[512]{0:T(512)}, f32[1,512,768]{2,1,0:T(8,128)S(1)}) fusion(f32[1,512,768]{2,1,0:T(8,128)} %copy-done.12, bf16[3072,768]{1,0:T(8,128)(2,1)} %param.19, bf16[768,3072]{1,0:T(8,128)(2,1)} %param.18, f32[768]{0:T(1024)} %get-tuple-element.86, f32[768]{0:T(1024)S(1)} %get-tuple-element.87, f32[512]{0:T(512)} %add_rsqrt_fusion.2, ...), kind=kOutput, calls=%fused_computation.213 | convolution fusion | flops 4850318848 | bytes 13384708 | tf_op jit(solution)/shard_map/dot_general | solution.py:129
  115.4 4.3 convolution_bitcast_fusion
  120.3 1.6 copy-done.6
  123.5 2.4 slice.185
  126.0 24.8 %all-gather.9.cloned.1.call-done = bf16[1,1024,12,64]{1,3,2,0:T(8,128)(2,1)} async-done(((bf16[1,512,12,64]{1,3,2,0:T(8,128)(2,1)}), bf16[1,1024,12,64]{1,3,2,0:T(8,128)(2,1)}) %all-gather.9.cloned.1.call-update) | async-done | bytes 1572880 | tf_op jit(solution)/shard_map/all_gather | solution.py:76
  150.8 12.5 %multiply_reduce_fusion.2 = (f32[12,512]{1,0:T(8,128)S(1)}, f32[12,512,1024]{2,1,0:T(8,128)}) fusion(bf16[1,1024,12,64]{1,3,2,0:T(8,128)(2,1)} %all-gather.9.cloned.1.call-done, bf16[512,12,32]{0,2,1:T(8,128)(2,1)S(1)} %get-tuple-element.109, bf16[512,12,32]{0,2,1:T(8,128)(2,1)S(1)} %get-tuple-element.108), kind=kOutput, calls=%fused_computation.13 | convolution fusion | flops 819456000 | bytes 27549696 | tf_op jit(solution)/shard_map/while/body/eval_jaxpr/sqhe,skhe->shqk/dot_general | solution.py:86
  163.3 14.9 %exponential_reduce_fusion = (f32[12,512]{1,0:T(8,128)S(1)}, f32[12,512]{1,0:T(8,128)}) fusion(f32[12,512,1024]{2,1,0:T(8,128)} %get-tuple-element.135, f32[12,512]{1,0:T(8,128)S(1)} %is-finite_select_fusion, f32[12,512]{1,0:T(8,128)S(1)} %get-tuple-element.134), kind=kLoop, calls=%fused_computation.4 | loop fusion | flops 31444992 | bytes 25264128 | tf_op jit(solution)/shard_map/while/body/eval_jaxpr/reduce_sum | solution.py:223
  180.0 11.4 %fusion.75 = bf16[12,64,512]{2,1,0:T(8,128)(2,1)S(1)} fusion(f32[12,512,1024]{2,1,0:T(8,128)} %get-tuple-element.135, f32[12,512]{1,0:T(8,128)} %get-tuple-element.74, f32[12,512]{1,0:T(8,128)} %copy-done.22, bf16[1,1024,1,12,64]{1,4,3,2,0:T(8,128)(2,1)} %all-gather.13.cloned.1.call-done), kind=kOutput, calls=%fused_computation.113 | convolution fusion | flops 830865408 | bytes 27574272 | tf_op jit(solution)/shard_map/while/body/eval_jaxpr/shqk,skhe->sqhe/dot_general | solution.py:90
  194.2 4.9 fusion.134
  199.2 6.3 fusion.19
  205.5 3.5 fusion.43
  209.3 5.7 fusion.42
  216.1 1.7 convolution_convert_fusion
  217.9 17.4 %multiply_reduce_fusion = (f32[12,512]{1,0:T(8,128)}, f32[12,512,1024]{2,1,0:T(8,128)}) fusion(f32[12,512,1024]{2,1,0:T(8,128)} %get-tuple-element.135, f32[12,512]{1,0:T(8,128)} %log_add_fusion, bf16[512,12,64]{0,2,1:T(8,128)(2,1)} %convolution_convert_fusion, bf16[1,1024,1,12,64]{1,4,3,2,0:T(8,128)(2,1)} %all-gather.13.cloned.1.call-done), kind=kOutput, calls=%fused_computation.2 | convolution fusion | flops 830466048 | bytes 52740096 | tf_op jit(solution)/shard_map/while/body/eval_jaxpr/sqhe,skhe->shqk/dot_general | solution.py:225
  235.3 16.8 %multiply_convert_fusion = bf16[12,512,1024]{2,1,0:T(8,128)(2,1)S(1)} fusion(f32[12,512,1024]{2,1,0:T(8,128)} %get-tuple-element.139, f32[12,512,1024]{2,1,0:T(8,128)} %get-tuple-element.135, f32[12,512]{1,0:T(8,128)} %get-tuple-element.138, f32[12,512]{1,0:T(8,128)} %log_add_fusion), kind=kLoop, calls=%fused_computation.1 | loop fusion | flops 31457280 | bytes 62963712 | tf_op jit(solution)/shard_map/while/body/eval_jaxpr/convert_element_type | solution.py:229
  252.1 4.6 copy-done.1
  256.7 4.0 multiply_bitcast_fusion
  261.8 13.5 %fusion.32 = f32[1,1024,12,64]{1,3,2,0:T(8,128)} fusion(bf16[512,12,64]{0,2,1:T(8,128)(2,1)S(1)} %copy-done.10, f32[12,512,1024]{2,1,0:T(8,128)} %get-tuple-element.135, f32[12,512]{1,0:T(8,128)} %log_add_fusion), kind=kOutput, calls=%fused_computation.53 | convolution fusion | flops 824180736 | bytes 29122560 | tf_op jit(solution)/shard_map/while/body/eval_jaxpr/shqk,sqhe->skhe/dot_general | solution.py:240
  276.4 3.6 fusion.91
  281.2 9.8 fusion.107
  291.6 8.9 fusion.132
  300.8 10.3 %multiply_bitcast_fusion.1 = f32[1,512,12,64]{1,3,2,0:T(8,128)} fusion(bf16[12,512,1024]{2,1,0:T(8,128)(2,1)} %copy-done.1, bf16[1,1024,12,64]{1,3,2,0:T(8,128)(2,1)} %all-gather.9.cloned.1.call-done), kind=kOutput, calls=%fused_computation.101 | convolution fusion | flops 805699584 | bytes 15728640 | tf_op jit(solution)/shard_map/while/body/eval_jaxpr/shqk,skhe->sqhe/dot_general | solution.py:231
  311.1 3.1 multiply_add_fusion.1
  315.3 34.4 %reduce-scatter.10.cloned.1.call-done = f32[1,512,12,64]{1,3,2,0:T(8,128)} async-done(((f32[1,1024,12,64]{1,3,2,0:T(8,128)}), f32[1,512,12,64]{1,3,2,0:T(8,128)}) %reduce-scatter.10.cloned.1.call-update) | async-done | bytes 1572880 | tf_op jit(solution)/shard_map/reduce_scatter | solution.py:262
  349.7 2.0 maximum_convert_fusion
  353.1 5.3 fusion.93
  358.5 5.2 fusion.45
  365.2 6.9 broadcast_multiply_fusion
  372.2 44.3 %reduce-scatter.14.cloned.1.call-done = f32[48,768]{1,0:T(8,128)} async-done(((f32[768,768]{1,0:T(8,128)}), f32[48,768]{1,0:T(8,128)}) %reduce-scatter.14.cloned.1.call-update) | async-done | bytes 147472 | tf_op jit(solution)/shard_map/reduce_scatter | solution.py:301
  416.5 115.0 %reduce-scatter.18.cloned.1.call-done = f32[192,768]{1,0:T(8,128)} async-done(((f32[3072,768]{1,0:T(8,128)}), f32[192,768]{1,0:T(8,128)}) %reduce-scatter.18.cloned.1.call-update) | async-done | bytes 589840 | tf_op jit(solution)/shard_map/reduce_scatter | solution.py:303
  531.5 115.2 %reduce-scatter.16.cloned.1.call-done = f32[48,3072]{1,0:T(8,128)} async-done(((f32[768,3072]{1,0:T(8,128)}), f32[48,3072]{1,0:T(8,128)}) %reduce-scatter.16.cloned.1.call-update) | async-done | bytes 589840 | tf_op jit(solution)/shard_map/reduce_scatter | solution.py:302
  646.8 94.2 %reduce-scatter.12.cloned.1.call-done = f32[48,2304]{1,0:T(8,128)} async-done(((f32[768,2304]{1,0:T(8,128)}), f32[48,2304]{1,0:T(8,128)}) %reduce-scatter.12.cloned.1.call-update) | async-done | bytes 442384 | tf_op jit(solution)/shard_map/reduce_scatter | solution.py:300
  741.0 149.3 %reduce-scatter.20.cloned.1.call-done = f32[48,4608]{1,0:T(8,128)} async-done(((f32[768,4608]{1,0:T(8,128)}), f32[48,4608]{1,0:T(8,128)}) %reduce-scatter.20.cloned.1.call-update) | async-done | bytes 884752 | tf_op jit(solution)/shard_map/reduce_scatter | solution.py:304
  891.6 59.5 %all-reduce = f32[4608]{0:T(1024)S(1)} all-reduce(f32[4608]{0:T(1024)S(1)} %reduce.43), channel_id=11, replica_groups=mesh['seq'=2,'batch'=16] {'batch'}, use_global_device_ids=true, to_apply=%region_36.37.clone | all-reduce | flops 4608 | bytes 36864
  951.2 5.5 psum.47
  956.7 3.5 fusion.48
  960.3 7.5 all-reduce.4.cloned.1.call-done
  967.7 1.9 copy.37
  969.7 1.6 copy.38
  (180 shorter events, 30.2 us)
Async XLA Ops:
  7.2 94.4 %copy-start = (bf16[768,768]{1,0:T(8,128)(2,1)S(1)}, bf16[768,768]{1,0:T(8,128)(2,1)}, u32[]{:S(2)}) copy-start(bf16[768,768]{1,0:T(8,128)(2,1)} %param.17) | copy-start | bytes 3538948
  7.2 54.0 %all-gather.7.cloned.1.call-start = ((), (), s32[]{:S(2)}) async-start(), calls=%async_computation.7 | async-start | bytes 2359296 | tf_op jit(solution)/shard_map/all_gather | solution.py:76
  12.2 4.1 copy-start.25
  16.9 5.8 copy-start.34
  16.9 98.4 %copy-start.23 = (f32[768]{0:T(1024)}, f32[768]{0:T(1024)S(1)}, u32[]{:S(2)}) copy-start(f32[768]{0:T(1024)S(1)} %get-tuple-element.89) | copy-start | bytes 9220
  16.9 5.8 copy-start.7
  27.0 2.1 copy-start.5
  31.1 59.4 %all-gather.11.cloned.1.call-start = ((), (), s32[]{:S(2)}) async-start(), calls=%async_computation.16 | async-start | bytes 2359296 | tf_op jit(solution)/shard_map/all_gather | solution.py:77
  33.6 117.2 %all-gather.9.cloned.1.call-start = ((), (), s32[]{:S(2)}) async-start(), calls=%async_computation.8 | async-start | bytes 2359296 | tf_op jit(solution)/shard_map/all_gather | solution.py:76
  115.1 4.7 copy-start.26
  115.4 4.4 copy-start.29
  119.7 2.1 copy-start.6
  119.8 2.1 copy-start.14
  119.8 2.1 copy-start.17
  123.4 56.6 %all-gather.13.cloned.1.call-start = ((), (), s32[]{:S(2)}) async-start(), calls=%async_computation.17 | async-start | bytes 2359296 | tf_op jit(solution)/shard_map/all_gather | solution.py:77
  125.9 185.2 %reduce-scatter.8.cloned.1.call-start = ((), (), s32[]{:S(2)}) async-start(), calls=%async_computation.9 | async-start | bytes 4718592 | tf_op jit(solution)/shard_map/reduce_scatter | solution.py:261
  163.3 14.9 %copy-start.22 = (f32[12,512]{1,0:T(8,128)}, f32[12,512]{1,0:T(8,128)S(1)}, u32[]{:S(2)}) copy-start(f32[12,512]{1,0:T(8,128)S(1)} %get-tuple-element.134) | copy-start | bytes 73732
  191.4 7.7 slice-start.2
  192.4 16.9 %copy-start.3 = (f32[1,512,768]{2,1,0:T(8,128)}, f32[1,512,768]{2,1,0:T(8,128)S(1)}, u32[]{:S(2)}) copy-start(f32[1,512,768]{2,1,0:T(8,128)S(1)} %get-tuple-element.99) | copy-start | bytes 4718596
  192.4 1.8 copy-start.37
  194.2 15.1 %copy-start.41 = (f32[512]{0:T(512)}, f32[512]{0:T(512)S(1)}, u32[]{:S(2)}) copy-start(f32[512]{0:T(512)S(1)} %add_rsqrt_fusion) | copy-start | bytes 6148
  194.2 4.9 copy-start.39
  194.2 4.9 slice-start.3
  194.2 4.9 copy-start.43
  194.2 11.3 %slice-start = ((s8[4718592]{0:T(1024)(128)(4,1)}), s8[4194304]{0:T(1024)(128)(4,1)S(1)}, s32[]{:S(2)}) async-start(s8[4718592]{0:T(1024)(128)(4,1)} %bitcast.215), calls=%async_computation.19 | async-start | bytes 8388608
  199.1 10.1 %copy-start.46 = (f32[512,3072]{1,0:T(8,128)}, f32[512,3072]{1,0:T(8,128)S(1)}, u32[]{:S(2)}) copy-start(f32[512,3072]{1,0:T(8,128)S(1)} %fusion.134) | copy-start | bytes 18874372
  199.2 6.4 slice-start.1
  205.5 3.5 copy-start.47
  252.1 4.6 copy-start.1
  260.7 89.1 %reduce-scatter.10.cloned.1.call-start = ((), (), s32[]{:S(2)}) async-start(), calls=%async_computation.10 | async-start | bytes 4718592 | tf_op jit(solution)/shard_map/reduce_scatter | solution.py:262
  275.3 141.2 %reduce-scatter.14.cloned.1.call-start = ((), (), s32[]{:S(2)}) async-start(), calls=%async_computation.12 | async-start | bytes 2506752 | tf_op jit(solution)/shard_map/reduce_scatter | solution.py:301
  280.1 251.5 %reduce-scatter.18.cloned.1.call-start = ((), (), s32[]{:S(2)}) async-start(), calls=%async_computation.14 | async-start | bytes 10027008 | tf_op jit(solution)/shard_map/reduce_scatter | solution.py:303
  291.0 355.8 %reduce-scatter.16.cloned.1.call-start = ((), (), s32[]{:S(2)}) async-start(), calls=%async_computation.13 | async-start | bytes 10027008 | tf_op jit(solution)/shard_map/reduce_scatter | solution.py:302
  300.5 10.6 %copy-start.15 = (f32[512,32]{0,1:T(8,128)S(1)}, f32[512,32]{0,1:T(8,128)}, u32[]{:S(2)}) copy-start(f32[512,32]{0,1:T(8,128)} %copy-done.13) | copy-start | bytes 196612
  300.5 10.6 %copy-start.18 = (f32[512,32]{0,1:T(8,128)S(1)}, f32[512,32]{0,1:T(8,128)}, u32[]{:S(2)}) copy-start(f32[512,32]{0,1:T(8,128)} %copy-done.16) | copy-start | bytes 196612
  300.5 440.5 %reduce-scatter.12.cloned.1.call-start = ((), (), s32[]{:S(2)}) async-start(), calls=%async_computation.11 | async-start | bytes 7520256 | tf_op jit(solution)/shard_map/reduce_scatter | solution.py:300
  349.7 3.4 copy-start.24
  349.7 3.4 copy-start.27
  349.7 3.4 copy-start.30
  349.7 3.4 copy-start.36
  358.4 531.9 %reduce-scatter.20.cloned.1.call-start = ((), (), s32[]{:S(2)}) async-start(), calls=%async_computation.15 | async-start | bytes 15040512 | tf_op jit(solution)/shard_map/reduce_scatter | solution.py:304
  363.7 1.4 copy-start.32
  363.7 1.5 copy-start.28
  372.1 518.2 %copy-start.45 = (u32[32]{0:T(128)S(1)}, u32[32]{0:T(128)}, u32[]{:S(2)}) copy-start(u32[32]{0:T(128)} %constant.139) | copy-start | bytes 388
  372.1 595.6 %all-reduce.4.cloned.1.call-start = ((), (), s32[]{:S(2)}) async-start(), calls=%async_computation.18 | async-start | bytes 5308416 | tf_op jit(solution)/shard_map/psum | solution.py:307
  967.7 3.5 copy-start.21
  967.7 4.4 copy-start.20
  967.7 5.2 copy-start.19
  (16 other events, 16.3 us)
Sparse Core Ops, SparseCore 0:
  31.2 29.8 all-gather.6
  63.3 27.1 all-gather.10
  123.6 27.1 all-gather.8
  152.8 27.1 all-gather.12
  260.8 43.3 reduce-scatter.7
  306.4 43.3 reduce-scatter.9
  353.5 62.9 reduce-scatter.13
  421.2 110.3 reduce-scatter.17
  535.6 111.0 reduce-scatter.15
  651.2 89.8 reduce-scatter.11
  745.2 145.0 reduce-scatter.19
  892.8 74.9 all-reduce.3
where the time goes:
time: 990 us; the launch traced here: 981 us
  waiting for transfers between devices  629 us (64%)
  matrix products  174 us (18%)
  blocking collectives  65.1 us (7%)
  other arithmetic  59.9 us (6%)
  local copies, waits for them, and re-layouts  35.4 us (4%)
  between operations  17.4 us (2%)
    reduce_scatter x1, waiting for transfers between devices, per_device(): lax.psum_scatter(grad_cond, 'batch', scatter_dimension=0, tiled=True)  149 us
    reduce_scatter x1, waiting for transfers between devices, per_device(): lax.psum_scatter(grad_up, 'batch', scatter_dimension=0, tiled=True)  115 us
    reduce_scatter x1, waiting for transfers between devices, per_device(): lax.psum_scatter(grad_down, 'batch', scatter_dimension=0, tiled=True)  115 us
    reduce_scatter x1, waiting for transfers between devices, per_device(): lax.psum_scatter(grad_mix, 'batch', scatter_dimension=0, tiled=True)  94.2 us
    unnamed x1, blocking collectives  59.5 us
    all_gather x2, waiting for transfers between devices, collect(): lax.all_gather(key_part, 'seq', axis=1, tiled=True)  51.7 us
    reduce_scatter x1, waiting for transfers between devices, per_device(): lax.psum_scatter(grad_project, 'batch', scatter_dimension=0, tiled=True)  44.3 us
    reduce_scatter x1, waiting for transfers between devices, per_device(): lax.psum_scatter(grad_value_all, 'seq', scatter_dimension=1, tiled=True)  34.4 us
  transfers between devices with their start and end apart: 12, of which 11 were waited for; matrix products, arithmetic and copies ran while one was open for 12% of the time, Pallas kernels for 0%

commit v1 on v0

v1 whole, which is shorter than its diff:
```python
import functools
import math

import jax
import jax.numpy as jnp
import numpy as np
from jax import lax
from jax.experimental import pallas as pl
from jax.experimental.pallas import tpu as pltpu
from jax.sharding import PartitionSpec as P

HEAD = 64
PAIR = 2 * HEAD
ITER = 2 * PAIR
EPS = 1e-06
THETA = 10000.0
LOG2E = 1.4426950408889634
SCALE = HEAD ** (-0.5)
EXP_SCALE = SCALE * LOG2E
GELU_A = math.sqrt(2.0 / math.pi)
GELU_B = 0.044715
BF = jnp.bfloat16
F32 = jnp.float32
MESH = pl.DeviceIdType.MESH
ROWS_LN = 128


def dot(left, right, left_dim=1, right_dim=0):
    return lax.dot_general(
        left, right, (((left_dim,), (right_dim,)), ((), ())), preferred_element_type=F32
    )


def lanes(shape):
    return lax.broadcasted_iota(jnp.int32, shape, len(shape) - 1)


def one_head(values, head):
    return jnp.where((lanes(values.shape) // HEAD) == head, values, jnp.zeros_like(values))


def bit_of(value, bit):
    return lax.rem(value // bit, 2)


def flip(value, bit):
    return value + bit - 2 * bit * bit_of(value, bit)


def aligned(value, unit):
    return pl.multiple_of(value, unit)


def rotary_constants(length):
    half_size = HEAD // 2
    freqs = THETA ** (-np.arange(half_size, dtype=np.float64) * 2.0 / HEAD)
    angles = np.arange(length, dtype=np.float64)[:, None] * freqs[None, :]
    cosine, sine = np.cos(angles), np.sin(angles)
    cosine = np.concatenate([cosine] * 4, axis=1).astype(np.float32)
    sine = np.concatenate([-sine, sine] * 2, axis=1).astype(np.float32)
    return cosine, sine


def swap_halves(values):
    first = lax.rem(lanes(values.shape), HEAD) < HEAD // 2
    return jnp.where(
        first, pltpu.roll(values, PAIR - HEAD // 2, 1), pltpu.roll(values, HEAD // 2, 1)
    )


def normalize(values):
    row_mean = jnp.mean(values, axis=-1, keepdims=True)
    centered = values - row_mean
    row_var = jnp.mean(centered * centered, axis=-1, keepdims=True)
    inverse = lax.rsqrt(row_var + EPS)
    return centered * inverse, inverse


def norm_back(grad_normed, normed, inverse):
    grad_mean = jnp.mean(grad_normed, axis=-1, keepdims=True)
    cross_mean = jnp.mean(grad_normed * normed, axis=-1, keepdims=True)
    return inverse * (grad_normed - grad_mean - normed * cross_mean)


def col_sum(values):
    return jnp.sum(values, axis=0, keepdims=True)


def bits_of(count):
    return [1 << k for k in range(count.bit_length() - 1)]


def wait_bytes(ref, sem):
    pltpu.make_async_copy(ref, ref, sem).wait()


class Job:
    def __init__(self, grad, out, first, width, seq_early, sizes):
        self.grad, self.out, self.first, self.width = grad, out, first, width
        self.seq_count, self.batch_count = sizes
        self.row_block = grad.shape[0] // self.batch_count
        self.fold = 1
        while self.row_block * self.fold % 16:
            self.fold *= 2
        self.unit = self.row_block * self.fold
        self.units = self.batch_count // self.fold
        halvings = [("batch", bit) for bit in bits_of(self.units)]
        if seq_early and self.fold == 1 and (width // self.seq_count) % PAIR == 0:
            self.stages = (
                halvings[:1]
                + [("cut", bit) for bit in bits_of(self.seq_count)]
                + halvings[1:]
                + [("gather", bit) for bit in bits_of(self.seq_count)[::-1]]
            )
        else:
            self.stages = (
                halvings
                + [("add", bit) for bit in bits_of(self.seq_count)]
                + [("fold", bit) for bit in bits_of(self.fold)]
            )

    def landing_shapes(self):
        count, width, shapes = self.units, self.width, []
        for kind, _ in self.stages:
            if kind == "batch":
                count //= 2
            elif kind == "cut":
                width //= 2
            shapes.append((count * self.unit, width))
            if kind == "gather":
                width *= 2
        return shapes


def job_list(grads, outs, sizes):
    grad_down, grad_up, grad_project, grad_mix = grads
    out_down, out_up, out_project, out_mix = outs
    model_width, hidden_width = grad_up.shape
    jobs = {}
    jobs["down_y"] = Job(grad_down, out_down, 0, ITER, False, sizes)
    jobs["down_x"] = Job(grad_down, out_down, ITER, model_width - ITER, True, sizes)
    jobs["up_y"] = Job(grad_up, out_up, 0, hidden_width // 2, False, sizes)
    jobs["up_x"] = Job(grad_up, out_up, hidden_width // 2, hidden_width // 2, True, sizes)
    jobs["project"] = Job(grad_project, out_project, 0, model_width, False, sizes)
    for i in range(model_width // ITER):
        jobs[f"mix{i}_x"] = Job(grad_mix, out_mix, i * 3 * ITER, 2 * ITER, True, sizes)
        jobs[f"mix{i}_y"] = Job(grad_mix, out_mix, i * 3 * ITER + 2 * ITER, ITER, False, sizes)
    return jobs


def step_kernel(
    sizes,
    seqs_here,
    pos_here,
    inputs_hbm,
    cot_hbm,
    codes_ref,
    bias_ref,
    cos_hbm,
    sin_hbm,
    mix_hbm,
    project_hbm,
    up_hbm,
    down_hbm,
    cond_hbm,
    layer_hbm,
    igrad_hbm,
    out_mix,
    out_project,
    out_up,
    out_down,
    out_all,
    mix,
    project,
    up,
    down,
    cos,
    sin,
    x16,
    cot,
    x,
    x1,
    a_in,
    q,
    kv,
    kv_other,
    mixed,
    branch,
    b_in,
    slope,
    hidden,
    gbf,
    gx,
    dout,
    dkv,
    lse,
    mod,
    codes_other,
    gsum,
    gsum_other,
    landings,
    load_sem,
    share_sem,
    share_recv,
    kv_sem,
    kv_recv,
    dkv_sem,
    dkv_recv,
    small_sem,
    small_recv,
    job_sem,
    job_recv,
):
    seq_count, batch_count = sizes
    rows, width = x.shape
    hidden_width = up.shape[1]
    pairs = width // PAIR
    iters = width // ITER
    block = 3 * ITER
    s = lax.axis_index("seq")
    b = lax.axis_index("batch")
    core = lax.rem(b, 2)
    core_peer = (s, flip(b, 1))

    barrier = pltpu.get_barrier_semaphore()
    peers = [(s, flip(b, bit)) for bit in bits_of(batch_count)]
    peers += [(flip(s, bit), b) for bit in bits_of(seq_count)]
    for peer in peers:
        pl.semaphore_signal(barrier, inc=1, device_id=peer, device_id_type=MESH)

    def share_peer(j):
        return core * seqs_here + j, b - core + s // seqs_here

    def is_self(j):
        ps, pb = share_peer(j)
        return jnp.logical_and(ps == s, pb == b)

    for j in range(seqs_here):

        @pl.when(jnp.logical_not(is_self(j)))
        def _():
            pl.semaphore_signal(barrier, inc=1, device_id=share_peer(j), device_id_type=MESH)

    own = jnp.where(s // seqs_here == core, 1, 0)

    cond_up = pltpu.make_async_copy(cond_hbm.at[:, pl.ds(0, hidden_width)], up, load_sem.at[0])
    cond_up.start()
    rest = cond_hbm.shape[1] - hidden_width
    cond_down = []
    for i in range(rest // width):
        cond_down.append(
            pltpu.make_async_copy(
                cond_hbm.at[:, pl.ds(hidden_width + i * width, width)],
                down.at[pl.ds(i * width, width), :],
                load_sem.at[1 + i],
            )
        )
        cond_down[-1].start()
    mix_loads = []
    for i in range(iters):
        for part in range(3):
            mix_loads.append(
                pltpu.make_async_copy(
                    mix_hbm.at[:, pl.ds(part * width + i * ITER, ITER)],
                    mix.at[:, pl.ds(i * block + part * ITER, ITER)],
                    load_sem.at[8],
                )
            )
            mix_loads[-1].start()
    row0 = core * rows
    load_cos = pltpu.make_async_copy(
        cos_hbm.at[pl.ds(aligned(row0, 128), rows), :], cos, load_sem.at[5]
    )
    load_sin = pltpu.make_async_copy(
        sin_hbm.at[pl.ds(aligned(row0, 128), rows), :], sin, load_sem.at[6]
    )
    load_project = pltpu.make_async_copy(project_hbm, project, load_sem.at[7])
    load_cos.start()
    load_sin.start()
    load_project.start()

    pl.semaphore_wait(barrier, len(peers) + seqs_here - own)

    def share_copy(source, target, j, k):
        return pltpu.make_async_remote_copy(
            src_ref=source,
            dst_ref=target,
            send_sem=share_sem.at[k],
            recv_sem=share_recv.at[k],
            device_id=share_peer(j),
            device_id_type=MESH,
        )

    slot = lax.rem(s, seqs_here)

    def share_start(source, target, k):
        for j in range(seqs_here):

            @pl.when(is_self(j))
            def _():
                pltpu.make_async_copy(source(j), target(slot), share_recv.at[k]).start()

            @pl.when(jnp.logical_not(is_self(j)))
            def _():
                share_copy(source(j), target(slot), j, k).start()

    def share_sent(source, target, k):
        for j in range(seqs_here):

            @pl.when(jnp.logical_not(is_self(j)))
            def _():
                share_copy(source(j), target(slot), j, k).wait_send()

    def rows_of(ref):
        return lambda j: ref.at[pl.ds(aligned(j * pos_here, 16), pos_here), :]

    def seq_of(ref):
        return lambda j: ref.at[j]

    def to_core(source, target, sems, recvs, k):
        return pltpu.make_async_remote_copy(
            src_ref=source,
            dst_ref=target,
            send_sem=sems.at[k],
            recv_sem=recvs.at[k],
            device_id=core_peer,
            device_id_type=MESH,
        )

    code_copy = to_core(codes_ref, codes_other, small_sem, small_recv, 0)
    code_copy.start()
    share_start(seq_of(inputs_hbm), rows_of(x16), 0)
    share_start(seq_of(cot_hbm), rows_of(cot), 1)

    code_copy.wait()
    own_f = own.astype(F32)
    code_rows = codes_ref[...] * own_f + codes_other[...] * (1.0 - own_f)
    row_ids = lax.broadcasted_iota(jnp.int32, code_rows.shape, 0)
    half_rows = code_rows.shape[0] // 2
    code = col_sum(jnp.where(row_ids == slot, code_rows, 0.0))
    flag = col_sum(jnp.where(row_ids == slot + half_rows, code_rows, 0.0))
    code_lhs = jnp.broadcast_to(code, (8, width)).astype(BF)
    cond_up.wait()
    for piece in range(hidden_width // width):
        at = slice(piece * width, (piece + 1) * width)
        mod[:, at] = dot(code_lhs, up[:, at]) + bias_ref[:, at]
    load_up = pltpu.make_async_copy(up_hbm, up, load_sem.at[0])
    load_up.start()
    for i in range(rest // width):
        cond_down[i].wait()
        at = slice(hidden_width + i * width, hidden_width + (i + 1) * width)
        mod[:, at] = dot(code_lhs, down[i * width : (i + 1) * width, :]) + bias_ref[:, at]
    load_down = pltpu.make_async_copy(down_hbm, down, load_sem.at[1])
    load_down.start()

    def piece_of(index, start=0, size=None):
        size = width if size is None else size
        return mod[0:1, pl.ds(index * width + start, size)]

    SHIFT_MIX, SCALE_MIX, GATE_MIX, SHIFT_FEED, SCALE_FEED, GATE_FEED = range(6)

    def norm_rows(source, target, shift_index, scale_index):
        def body(i, _):
            at = pl.ds(aligned(i * ROWS_LN, ROWS_LN), ROWS_LN)
            normed, _ = normalize(source[at, :].astype(F32))
            target[at, :] = (
                normed * (1.0 + piece_of(scale_index)) + piece_of(shift_index)
            ).astype(BF)
            return 0

        lax.fori_loop(0, rows // ROWS_LN, body, 0)

    def rotate(values, sign):
        parts = []
        for p in range(values.shape[1] // PAIR):
            part = values[:, p * PAIR : (p + 1) * PAIR]
            parts.append(part * cos[...] + sign * (swap_halves(part) * sin[...]))
        return jnp.concatenate(parts, axis=1)

    def project_part(part, target, base):
        def body(i, _):
            made = dot(a_in[...], mix[:, pl.ds(aligned(i * block + part * ITER, ITER), ITER)])
            if part < 2:
                made = rotate(made, 1.0)
            target[:, pl.ds(aligned(base + i * ITER, ITER), ITER)] = made.astype(BF)
            return 0

        lax.fori_loop(0, iters, body, 0)

    def kv_copy(which, part):
        at = pl.ds(part * width, width)
        return to_core(kv.at[:, at], kv_other.at[which, :, at], kv_sem, kv_recv, 2 * which + part)

    def attend(which):
        group = pairs // 2

        def body(i, _):
            for inner in range(group):
                pair = i * group + inner
                at = pl.ds(aligned(pair * PAIR, PAIR), PAIR)
                at_v = pl.ds(aligned(width + pair * PAIR, PAIR), PAIR)
                query = q[:, at]
                key = jnp.concatenate([kv[:, at], kv_other[which, :, at]], axis=0)
                value = jnp.concatenate([kv[:, at_v], kv_other[which, :, at_v]], axis=0)
                outs = []
                for head in range(2):
                    scores = dot(one_head(query, head), key, 1, 1)
                    top = jnp.max(scores, axis=1, keepdims=True)
                    weights = jnp.exp2((scores - top) * EXP_SCALE)
                    ones = jnp.where(
                        (lanes(value.shape) // HEAD) == head, value, jnp.ones_like(value)
                    )
                    made = dot(weights.astype(BF), ones)
                    total = made[:, HEAD * (1 - head) : HEAD * (1 - head) + 1]
                    outs.append(made * (1.0 / total))
                    if which == 1:
                        level = top * EXP_SCALE + jnp.log2(total)
                        lse[...] = jnp.where(
                            lanes(lse.shape) == 2 * pair + head, level, lse[...]
                        )
                mixed[:, at] = jnp.where(
                    lanes(outs[0].shape) < HEAD, outs[0], outs[1]
                ).astype(BF)
            return 0

        lax.fori_loop(0, 2, body, 0)

    def forward(which):
        if which == 0:
            wait_bytes(x16, share_recv.at[0])
        norm_rows(x16 if which == 0 else x, a_in, SHIFT_MIX, SCALE_MIX)
        if which == 0:
            for load in mix_loads:
                load.wait()
            load_cos.wait()
            load_sin.wait()
        project_part(1, kv, 0)
        key_copy = kv_copy(which, 0)
        key_copy.start()
        project_part(2, kv, width)
        value_copy = kv_copy(which, 1)
        value_copy.start()
        project_part(0, q, 0)
        key_copy.wait()
        value_copy.wait()
        attend(which)
        if which == 0:
            load_project.wait()

        def mix_out(i, _):
            at = pl.ds(aligned(i * ITER, ITER), ITER)
            made = dot(mixed[...], project[:, at])
            if which == 1:
                branch[:, at] = made.astype(BF)
            base = x16[:, at].astype(F32) if which == 0 else x[:, at]
            gate = mod[0:1, pl.ds(aligned(GATE_MIX * width + i * ITER, ITER), ITER)]
            x1[:, at] = base + gate * made
            return 0

        lax.fori_loop(0, iters, mix_out, 0)
        norm_rows(x1, b_in, SHIFT_FEED, SCALE_FEED)
        if which == 0:
            load_up.wait()
        step = 2 * ITER

        def feed_up(i, _):
            at = pl.ds(aligned(i * step, step), step)
            pre = dot(b_in[...], up[:, at])
            square = pre * pre
            inner = jnp.tanh(pre * (GELU_A + (GELU_A * GELU_B) * square))
            left = 0.5 * (1.0 + inner)
            hidden[:, at] = (pre * left).astype(BF)
            if which == 1:
                bend = GELU_A + (3.0 * GELU_A * GELU_B) * square
                slope[:, at] = (left + (0.5 * pre) * (1.0 - inner * inner) * bend).astype(BF)
            return 0

        lax.fori_loop(0, hidden_width // step, feed_up, 0)
        if which == 0:
            load_down.wait()

        def feed_down(i, _):
            at = pl.ds(aligned(i * ITER, ITER), ITER)
            made = dot(hidden[...], down[:, at])
            gate = mod[0:1, pl.ds(aligned(GATE_FEED * width + i * ITER, ITER), ITER)]
            result = x1[:, at] + gate * made
            if which == 0:
                x[:, at] = x16[:, at].astype(F32) + flag[:, 0:1] * result
            else:
                x16[:, at] = result.astype(BF)
                grad = cot[:, at].astype(F32)
                mod[1:2, pl.ds(aligned(GATE_FEED * width + i * ITER, ITER), ITER)] = col_sum(
                    grad * made
                )
                gbf[:, at] = (gate * grad).astype(BF)
            return 0

        lax.fori_loop(0, iters, feed_down, 0)

    forward(0)
    share_sent(seq_of(inputs_hbm), rows_of(x16), 0)
    wait_bytes(cot, share_recv.at[1])
    share_sent(seq_of(cot_hbm), rows_of(cot), 1)
    forward(1)
    share_start(rows_of(x16), seq_of(layer_hbm), 2)

    jobs = job_list((down, up, project, mix), (out_down, out_up, out_project, out_mix), sizes)
    landing_at, sem_at = 0, 0
    for job in jobs.values():
        job.landing = landings[landing_at : landing_at + len(job.stages)]
        job.sem_base = sem_at
        landing_at += len(job.stages)
        sem_at += len(job.stages)

    def job_view(job, stage):
        stride, start, wide = 1, job.first, job.width
        for kind, bit in job.stages[:stage]:
            if kind == "batch":
                stride = 2 * bit
            elif kind == "cut":
                wide //= 2
                start = start + bit_of(s, bit) * wide
        return stride, start, wide

    def gather_view(job, stage):
        start, wide = job.first, job.width
        done = [bit for kind, bit in job.stages[:stage] if kind == "gather"]
        for kind, bit in job.stages:
            if kind == "cut" and bit not in done:
                wide //= 2
                start = start + bit_of(s, bit) * wide
        return start, wide

    def job_copies(job, stage):
        kind, bit = job.stages[stage]
        land = job.landing[stage]
        height, fold = job.unit, job.fold
        me = b // fold
        k = job.sem_base + stage
        copies = []

        def add(row, start, wide, target, peer):
            source = job.grad.at[
                pl.ds(aligned(row * height, height), height), pl.ds(aligned(start, PAIR), wide)
            ]
            copies.append(
                pltpu.make_async_remote_copy(
                    src_ref=source,
                    dst_ref=target,
                    send_sem=job_sem.at[k],
                    recv_sem=job_recv.at[k],
                    device_id=peer,
                    device_id_type=MESH,
                )
            )

        stride, start, wide = job_view(job, stage)
        if kind == "batch":
            for t in range(job.units // (2 * bit)):
                row = lax.rem(me, bit) + (1 - bit_of(me, bit)) * bit + t * 2 * bit
                there = land.at[pl.ds(t * height, height), :]
                add(row, start, wide, there, (s, flip(b, bit * fold)))
        elif kind == "cut":
            half = wide // 2
            for t in range(job.units // stride):
                row = lax.rem(me, stride) + t * stride
                add(
                    row,
                    start + (1 - bit_of(s, bit)) * half,
                    half,
                    land.at[pl.ds(t * height, height), :],
                    (flip(s, bit), b),
                )
        elif kind == "add":
            add(me, start, wide, land, (flip(s, bit), b))
        elif kind == "fold":
            add(me, start, wide, land, (s, flip(b, bit)))
        else:
            start, wide = gather_view(job, stage)
            add(me, start, wide, land, (flip(s, bit), b))
        return copies

    def job_start(name, stage):
        for copy in job_copies(jobs[name], stage):
            copy.start()

    def job_finish(name, stage):
        job = jobs[name]
        kind, bit = job.stages[stage]
        land = job.landing[stage]
        height = job.unit
        me = b // job.fold
        k = job.sem_base + stage
        wait_bytes(land, job_recv.at[k])
        wait_bytes(land, job_sem.at[k])
        stride, start, wide = job_view(job, stage)
        last = stage == len(job.stages) - 1
        if kind in ("batch", "cut"):
            if kind == "batch":
                stride = 2 * bit
            else:
                wide //= 2
                start = start + bit_of(s, bit) * wide

            def body(t, _):
                row = lax.rem(me, stride) + t * stride
                at = pl.ds(aligned(row * height, height), height)
                cols = pl.ds(aligned(start, PAIR), wide)
                from_there = land[pl.ds(aligned(t * height, height), height), :].astype(F32)
                job.grad[at, cols] = (job.grad[at, cols].astype(F32) + from_there).astype(BF)
                return 0

            lax.fori_loop(0, job.units // stride, body, 0)
        elif kind in ("add", "fold"):
            at = pl.ds(aligned(me * height, height), height)
            cols = pl.ds(start, wide)
            total = job.grad[at, cols].astype(F32) + land[...].astype(F32)
            if last:
                mine = total[: job.row_block]
                for n in range(1, job.fold):
                    here = total[n * job.row_block : (n + 1) * job.row_block]
                    mine = jnp.where(lax.rem(b, job.fold) == n, here, mine)
                job.out[:, cols] = mine
            else:
                job.grad[at, cols] = total.astype(BF)
        else:
            start, wide = gather_view(job, stage)
            at = pl.ds(aligned(me * height, height), height)
            theirs = start + (1 - 2 * bit_of(s, bit)) * wide
            if last:
                cols = pl.ds(aligned(start, PAIR), wide)
                job.out[:, cols] = job.grad[at, cols].astype(F32)
                job.out[:, pl.ds(aligned(theirs, PAIR), wide)] = land[...].astype(F32)
            else:
                job.grad[at, pl.ds(aligned(theirs, PAIR), wide)] = land[...]
        if not last:
            job_start(name, stage + 1)

    step = width

    def feed_back(i, _):
        at = pl.ds(aligned(i * step, step), step)
        grad_hidden = dot(gbf[...], down[at, :], 1, 1)
        grad_pre = (grad_hidden * slope[:, at].astype(F32)).astype(BF)
        down[at, :] = dot(hidden[:, at], gbf[...], 0, 0).astype(BF)
        hidden[:, at] = grad_pre
        return 0

    lax.fori_loop(0, hidden_width // step, feed_back, 0)
    job_start("down_y", 0)
    job_start("down_x", 0)

    def feed_back_in(i, _):
        at = pl.ds(aligned(i * ITER, ITER), ITER)
        gx[:, at] = dot(hidden[...], up[at, :], 1, 1)
        return 0

    lax.fori_loop(0, iters, feed_back_in, 0)
    job_finish("down_y", 0)
    job_finish("down_x", 0)

    def feed_up_grad(i, _):
        at = pl.ds(aligned(i * step, step), step)
        up[:, at] = dot(b_in[...], hidden[:, at], 0, 0).astype(BF)
        return 0

    lax.fori_loop(0, hidden_width // step, feed_up_grad, 0)
    job_start("up_y", 0)
    job_start("up_x", 0)

    def middle_rows(i, sums):
        at = pl.ds(aligned(i * ROWS_LN, ROWS_LN), ROWS_LN)
        normed, inverse = normalize(x1[at, :])
        grad_in = gx[at, :]
        made = cot[at, :].astype(F32) + norm_back(
            grad_in * (1.0 + piece_of(SCALE_FEED)), normed, inverse
        )
        gx[at, :] = made
        gbf[at, :] = (piece_of(GATE_MIX) * made).astype(BF)
        return (
            sums[0] + col_sum(grad_in),
            sums[1] + col_sum(grad_in * normed),
            sums[2] + col_sum(made * branch[at, :].astype(F32)),
        )

    zero = jnp.zeros((1, width), F32)
    sums = lax.fori_loop(0, rows // ROWS_LN, middle_rows, (zero, zero, zero))
    for index, total in zip((SHIFT_FEED, SCALE_FEED, GATE_MIX), sums):
        mod[1:2, pl.ds(index * width, width)] = total

    def project_back(i, _):
        at = pl.ds(aligned(i * ITER, ITER), ITER)
        dout[:, at] = dot(gbf[...], project[at, :], 1, 1).astype(BF)
        return 0

    lax.fori_loop(0, iters, project_back, 0)
    project[...] = dot(mixed[...], gbf[...], 0, 0).astype(BF)
    job_start("project", 0)
    job_finish("up_y", 0)
    job_finish("up_x", 0)
    x1[...] = jnp.zeros_like(x1)

    def dkv_copy(i):
        at = pl.ds(aligned(i * 2 * ITER, 2 * ITER), 2 * ITER)
        there = pl.ds(aligned(2 * width + i * 2 * ITER, 2 * ITER), 2 * ITER)
        return to_core(slope.at[:, at], slope.at[:, there], dkv_sem, dkv_recv, i)

    def attend_back(i):
        for inner in range(2):
            pair = 2 * i + inner
            at = pl.ds(aligned(pair * PAIR, PAIR), PAIR)
            at_v = pl.ds(aligned(width + pair * PAIR, PAIR), PAIR)
            query, grads = q[:, at], dout[:, at]
            key = jnp.concatenate([kv[:, at], kv_other[1, :, at]], axis=0)
            value = jnp.concatenate([kv[:, at_v], kv_other[1, :, at_v]], axis=0)
            crossed = grads.astype(F32) * mixed[:, at].astype(F32)
            lane_q, lane_k = lanes(query.shape), lanes(key.shape)
            dq = dk = dv = None
            for head in range(2):
                spare = HEAD * (1 - head)
                query_h, grads_h = one_head(query, head), one_head(grads, head)
                key_h = one_head(key, head)
                level = jnp.sum(
                    jnp.where(lanes(lse.shape) == 2 * pair + head, lse[...], 0.0),
                    axis=1,
                    keepdims=True,
                )
                delta = jnp.sum(one_head(crossed, head), axis=1, keepdims=True)
                scaled = query_h.astype(F32) * EXP_SCALE
                high = scaled.astype(BF)
                low = (scaled - high.astype(F32)).astype(BF)
                level1 = (-level).astype(BF)
                left = -level - level1.astype(F32)
                level2 = left.astype(BF)
                level3 = (left - level2.astype(F32)).astype(BF)
                low = jnp.where(lane_q == spare, level1, low)
                low = jnp.where(lane_q == spare + 1, level2, low)
                low = jnp.where(lane_q == spare + 2, level3, low)
                key_low = jnp.where(
                    jnp.logical_and(lane_k >= spare, lane_k < spare + 3),
                    jnp.ones_like(key),
                    key_h,
                )
                probs = jnp.exp2(
                    dot(
                        jnp.concatenate([high, low], axis=1),
                        jnp.concatenate([key_h, key_low], axis=1),
                        1,
                        1,
                    )
                )
                delta1 = (-delta).astype(BF)
                delta2 = (-delta - delta1.astype(F32)).astype(BF)
                grads_d = jnp.where(lane_q == spare, delta1, grads_h)
                grads_d = jnp.where(lane_q == spare + 1, delta2, grads_d)
                value_d = jnp.where(
                    jnp.logical_and(lane_k >= spare, lane_k < spare + 2),
                    jnp.ones_like(value),
                    value,
                )
                grad_scores = (probs * dot(grads_d, value_d, 1, 1)).astype(BF)
                dv_h = dot(probs.astype(BF), grads_h, 0, 0)
                dk_h = dot(grad_scores, query_h, 0, 0)
                dq_h = dot(grad_scores, key_h)
                if head == 0:
                    dq, dk, dv = dq_h, dk_h, dv_h
                else:
                    dq, dk, dv = dq + dq_h, dk + dk_h, dv + dv_h
            hidden[:, pl.ds(aligned(i * block + inner * PAIR, PAIR), PAIR)] = rotate(
                dq * SCALE, -1.0
            ).astype(BF)
            for part, made in ((0, dk * SCALE), (1, dv)):
                off = part * ITER + inner * PAIR
                dkv[lax.rem(i, 2), :, pl.ds(off, PAIR)] = made[:rows]
                slope[:, pl.ds(aligned(i * 2 * ITER + off, PAIR), PAIR)] = made[rows:].astype(BF)

    def attend_finish(i):
        copy = dkv_copy(i)
        copy.wait()
        there = 2 * width + i * 2 * ITER
        dk = dkv[i % 2, :, 0:ITER] + slope[:, pl.ds(there, ITER)].astype(F32)
        dv = dkv[i % 2, :, ITER : 2 * ITER] + slope[:, pl.ds(there + ITER, ITER)].astype(F32)
        hidden[:, pl.ds(i * block + ITER, ITER)] = rotate(dk, -1.0).astype(BF)
        hidden[:, pl.ds(i * block + 2 * ITER, ITER)] = dv.astype(BF)
        here = pl.ds(i * block, block)
        x1[...] += dot(hidden[:, here], mix[:, here], 1, 1)
        mix[:, here] = dot(a_in[...], hidden[:, here], 0, 0).astype(BF)
        job_start(f"mix{i}_x", 0)
        job_start(f"mix{i}_y", 0)

    def attend_step(i, _):
        attend_back(i)
        dkv_copy(i).start()

        @pl.when(i == 0)
        def _():
            job_finish("project", 0)
            job_finish("down_x", 1)
            job_finish("down_y", 1)

        for done in range(1, iters):

            @pl.when(i == done)
            def _():
                attend_finish(done - 1)
                if done == 1:
                    job_finish("down_x", 2)
                    job_finish("down_y", 2)
                    job_finish("up_x", 1)
                if done == 2:
                    job_finish("up_y", 1)
                    job_finish("down_x", 3)
                    job_finish("down_y", 3)
                    job_finish("up_x", 2)
                    job_finish("mix0_x", 0)
                    job_finish("mix0_y", 0)
                    job_finish("project", 1)

        return 0

    lax.fori_loop(0, iters, attend_step, 0)
    attend_finish(iters - 1)
    finished = {
        "down_x": 3, "down_y": 3, "up_x": 2, "up_y": 1, "project": 1, "mix0_x": 0, "mix0_y": 0
    }

    def last_rows(i, sums):
        at = pl.ds(aligned(i * ROWS_LN, ROWS_LN), ROWS_LN)
        normed, inverse = normalize(x[at, :])
        grad_in = x1[at, :]
        made = gx[at, :] + norm_back(grad_in * (1.0 + piece_of(SCALE_MIX)), normed, inverse)
        gbf[at, :] = made.astype(BF)
        return sums[0] + col_sum(grad_in), sums[1] + col_sum(grad_in * normed)

    sums = lax.fori_loop(0, rows // ROWS_LN, last_rows, (zero, zero))
    share_start(rows_of(gbf), seq_of(igrad_hbm), 3)
    for index, total in zip((SHIFT_MIX, SCALE_MIX), sums):
        mod[1:2, pl.ds(index * width, width)] = total

    strips = width // 128
    for strip in range(6 * strips):
        gsum[strip : strip + 1, :] = mod[1:2, strip * 128 : (strip + 1) * 128]
    for strip in range(strips):
        gsum[6 * strips + strip : 6 * strips + strip + 1, :] = code[
            :, strip * 128 : (strip + 1) * 128
        ]
    gsum[7 * strips :, :] = jnp.zeros_like(gsum[7 * strips :, :])
    gcopy = to_core(gsum, gsum_other, small_sem, small_recv, 1)
    gcopy.start()
    gcopy.wait()
    line_ids = lax.broadcasted_iota(jnp.int32, gsum.shape, 0)
    chip = b // 2
    gsum_other[...] = jnp.where(line_ids < 6 * strips, gsum[...] + gsum_other[...], gsum[...])
    keep = pltpu.make_async_copy(
        gsum_other, out_all.at[chip * seq_count + s], small_recv.at[0]
    )
    keep.start()
    keep.wait()

    def gather_copies():
        k = 2
        copies = []
        for bit in bits_of(seq_count):
            start = chip * seq_count + (s // bit) * bit
            copies.append((start, bit, (flip(s, bit), b)))
        for bit in bits_of(batch_count)[1:]:
            chips = bit // 2
            start = (chip // chips) * chips * seq_count
            copies.append((start, chips * seq_count, (s, flip(b, bit))))
        made = []
        for start, count, peer in copies:
            ref = out_all.at[pl.ds(start, count)]
            made.append(
                pltpu.make_async_remote_copy(
                    src_ref=ref,
                    dst_ref=ref,
                    send_sem=small_sem.at[k],
                    recv_sem=small_recv.at[k],
                    device_id=peer,
                    device_id_type=MESH,
                )
            )
            k += 1
        return made

    gathers = gather_copies()
    gathers[0].start()

    order = []
    longest = max(len(job.stages) for job in jobs.values())
    for late in range(longest + 12):
        for n, name in enumerate(jobs):
            stage = late - n // 2
            if finished.get(name, -1) < stage < len(jobs[name].stages) and stage >= 0:
                order.append((name, stage))
    gather_done = 0
    for n, (name, stage) in enumerate(order):
        job_finish(name, stage)
        if n % 4 == 3 and gather_done < len(gathers):
            gathers[gather_done].wait()
            gather_done += 1
            if gather_done < len(gathers):
                gathers[gather_done].start()
    while gather_done < len(gathers):
        gathers[gather_done].wait()
        gather_done += 1
        if gather_done < len(gathers):
            gathers[gather_done].start()
    wait_bytes(layer_hbm, share_recv.at[2])
    share_sent(rows_of(x16), seq_of(layer_hbm), 2)
    wait_bytes(igrad_hbm, share_recv.at[3])
    share_sent(rows_of(gbf), seq_of(igrad_hbm), 3)


def per_device(sizes, inputs, cotangent, cond_mask, timestep, embed_table, mix_weight,
               project_weight, up_weight, down_weight, cond_weight, cond_bias):
    seq_count, batch_count = sizes
    seqs_here, pos_here, width = inputs.shape
    hidden_width = up_weight.shape[1]
    length = pos_here * seq_count
    rows = seqs_here * pos_here
    code_rows = -(-seqs_here // 8) * 8
    pad = code_rows - seqs_here
    code = jax.nn.silu(embed_table[timestep]).astype(BF).astype(F32)
    flags = jnp.broadcast_to(cond_mask.astype(F32)[:, None], code.shape)
    codes = jnp.concatenate(
        [jnp.pad(code, ((0, pad), (0, 0))), jnp.pad(flags, ((0, pad), (0, 0)))], axis=0
    )
    cosine, sine = rotary_constants(length)
    shares = [
        jax.ShapeDtypeStruct((weight.shape[0] // batch_count, weight.shape[1]), F32)
        for weight in (mix_weight, project_weight, up_weight, down_weight)
    ]
    total = batch_count * seqs_here
    lines = -(-7 * (width // 128) // 8) * 8
    shells = [
        jax.ShapeDtypeStruct(weight.shape, BF)
        for weight in (down_weight, up_weight, project_weight, mix_weight)
    ]
    landings, sem_count = [], 0
    for job in job_list(shells, [None] * 4, sizes).values():
        landings += [pltpu.VMEM(shape, BF) for shape in job.landing_shapes()]
        sem_count += len(job.stages)
    vmem = pl.BlockSpec(memory_space=pltpu.VMEM)
    hbm = pl.BlockSpec(memory_space=pl.ANY)
    wide = (rows, width)
    smalls = 1 + len(bits_of(seq_count)) + len(bits_of(batch_count))
    dma = pltpu.SemaphoreType.DMA
    layer, igrad, share_mix, share_project, share_up, share_down, gall = pl.pallas_call(
        functools.partial(step_kernel, sizes, seqs_here, pos_here),
        name="block_step",
        out_shape=[
            jax.ShapeDtypeStruct(inputs.shape, BF),
            jax.ShapeDtypeStruct(inputs.shape, BF),
            *shares,
            jax.ShapeDtypeStruct((total, lines, 128), F32),
        ],
        in_specs=[hbm, hbm, vmem, vmem] + [hbm] * 7,
        out_specs=[hbm, hbm] + [vmem] * 4 + [vmem if total <= 32 else hbm],
        scratch_shapes=[
            pltpu.VMEM(mix_weight.shape, BF),
            pltpu.VMEM(project_weight.shape, BF),
            pltpu.VMEM(up_weight.shape, BF),
            pltpu.VMEM(down_weight.shape, BF),
            pltpu.VMEM((rows, PAIR), F32),
            pltpu.VMEM((rows, PAIR), F32),
            pltpu.VMEM(wide, BF),
            pltpu.VMEM(wide, BF),
            pltpu.VMEM(wide, F32),
            pltpu.VMEM(wide, F32),
            pltpu.VMEM(wide, BF),
            pltpu.VMEM(wide, BF),
            pltpu.VMEM((rows, 2 * width), BF),
            pltpu.VMEM((2, rows, 2 * width), BF),
            pltpu.VMEM(wide, BF),
            pltpu.VMEM(wide, BF),
            pltpu.VMEM(wide, BF),
            pltpu.VMEM((rows, hidden_width), BF),
            pltpu.VMEM((rows, hidden_width), BF),
            pltpu.VMEM(wide, BF),
            pltpu.VMEM(wide, F32),
            pltpu.VMEM(wide, BF),
            pltpu.VMEM((2, rows, 2 * ITER), F32),
            pltpu.VMEM((rows, 128), F32),
            pltpu.VMEM((8, 6 * width), F32),
            pltpu.VMEM(codes.shape, F32),
            pltpu.VMEM((lines, 128), F32),
            pltpu.VMEM((lines, 128), F32),
            landings,
            dma((9,)),
            dma((4,)),
            dma((4,)),
            dma((4,)),
            dma((4,)),
            dma((width // ITER,)),
            dma((width // ITER,)),
            dma((smalls,)),
            dma((smalls,)),
            dma((sem_count,)),
            dma((sem_count,)),
        ],
        compiler_params=pltpu.CompilerParams(
            collective_id=0, has_side_effects=True, vmem_limit_bytes=VMEM_BYTES
        ),
    )(
        inputs,
        cotangent,
        codes,
        cond_bias[None, :],
        jnp.asarray(cosine),
        jnp.asarray(sine),
        mix_weight,
        project_weight,
        up_weight,
        down_weight,
        cond_weight,
    )
    share_mix = (
        share_mix.reshape(share_mix.shape[0], width // ITER, 3, ITER)
        .transpose(0, 2, 1, 3)
        .reshape(share_mix.shape)
    )
    strips = width // 128
    grad_mod = gall[:, : 6 * strips].reshape(total, 6 * width)
    codes_all = gall[:, 6 * strips : 7 * strips].reshape(total, width)
    me = lax.axis_index("batch")
    code_rows_here = lax.dynamic_slice_in_dim(
        codes_all, me * (width // batch_count), width // batch_count, 1
    )
    share_cond = jnp.dot(code_rows_here.T, grad_mod, precision=lax.Precision.HIGHEST)
    share_bias = jnp.sum(
        lax.dynamic_slice_in_dim(
            grad_mod, me * (6 * width // batch_count), 6 * width // batch_count, 1
        ),
        axis=0,
    )
    return (
        layer,
        igrad.astype(F32),
        share_mix,
        share_project,
        share_up,
        share_down,
        share_cond,
        share_bias,
    )


VMEM_BYTES = 64 * 1024 * 1024 - 512 * 1024


def solution(mesh):
    sizes = (mesh.shape["seq"], mesh.shape["batch"])
    split = P("batch", "seq", None)
    placed = (split, split, P("batch"), P("batch")) + (P(),) * 7
    return jax.shard_map(
        functools.partial(per_device, sizes),
        mesh=mesh,
        in_specs=placed,
        out_specs=(split, split) + (P("batch", None),) * 5 + (P("batch"),),
        check_vma=False,
    )
```

time: 990 us -> 194 us (0.20)
  waiting for transfers between devices: 629 us -> 0 us
  Pallas kernels: 0 us -> 178 us
  matrix products: 174 us -> 1.88 us
  blocking collectives: 65.1 us -> 0 us
  other arithmetic: 59.9 us -> 4.64 us
  local copies, waits for them, and re-layouts: 35.4 us -> 7.17 us
  between operations: 17.4 us -> 2.04 us
    reduce_scatter x7 -> x0, waiting for transfers between devices: 553 us -> none  [the longest x1 149 us: per_device(): lax.psum_scatter(grad_cond, 'batch', scatter_dimension=0, tiled=True)]
    pallas_call x0 -> x1, Pallas kernels: none -> 178 us  [per_device(): pl.pallas_call(functools.partial(step_kernel, sizes, seqs_here, pos_here)...]
    dot_general x23 -> x1, matrix products: 160 us -> 1.88 us  [per_device(): jnp.dot(code_rows_here.T, grad_mod, precision=lax.Precision.HIGHEST)]
    all_gather x4 -> x0, waiting for transfers between devices: 68.9 us -> none  [the longest x2 51.7 us: collect(): lax.all_gather(key_part, 'seq', axis=1, tiled=True)]
    unnamed x1 -> x0, blocking collectives: 59.5 us -> none
    unnamed x117 -> x16, local copies, waits for them, and re-layouts: 29.6 us -> 3.26 us
    reduce_sum x8 -> x1, other arithmetic: 19.1 us -> 0.67 us  [per_device(): jnp.sum(lax.dynamic_slice_in_dim(grad_mod, me * (6 * width // batch_count...]
    convert_element_type x4 -> x2, other arithmetic: 18.8 us -> 3.2 us  [the longest x1 2.43 us: per_device(): igrad.astype(F32)]
  transfers between devices with their start and end apart: 12 -> 0, of which waited for: 11 -> 0; matrix products, arithmetic and copies ran while one was open for 12% -> 0% of each run, Pallas kernels for 0% -> 0%
where the time goes in v1:
time: 194 us
  Pallas kernels  178 us (92%)
  local copies, waits for them, and re-layouts  7.17 us (4%)
  other arithmetic  4.64 us (2%)
  between operations  2.04 us (1%)
    pallas_call x1, Pallas kernels, per_device(): pl.pallas_call(functools.partial(step_kernel, sizes, seqs_here, pos_here)...  178 us

profile of v1, /device:TPU:0, one launch (start us, length us, event | category | flops | bytes accessed | tf_op | source)
XLA Modules:
  0.0 193.8 jit_solution(12983396268310598243)
XLA Ops:
  1.3 0.8 fusion.2
  2.7 0.1 compare_select_fusion
  2.8 0.7 pad_maximum_fusion.codes_ref
  3.5 1.3 broadcast_in_dim.5.bias_ref
  4.8 178.1 %block_step.1 = (bf16[1,512,768]{2,1,0:T(8,128)(2,1)}, bf16[1,512,768]{2,1,0:T(8,128)(2,1)}, f32[48,2304]{1,0:T(8,128)}, f32[48,768]{1,0:T(8,128)}, f32[48,3072]...) custom-call(bf16[1,512,768]{2,1,0:T(8,128)(2,1)} %inputs_hbm.1, bf16[1,512,768]{2,1,0:T(8,128)(2,1)} %cot_hbm.1, ...), custom_call_target="tpu_custom_call" | custom-call | tf_op jit(solution)/shard_map/block_step/pallas_call | solution.py:949
  182.9 0.0 copy-start.3
  182.9 2.4 %convert_element_type.31 = f32[1,512,768]{2,1,0:T(8,128)} convert(bf16[1,512,768]{2,1,0:T(8,128)(2,1)} %get-tuple-element.16) | non-fusion elementwise | flops 393216 | bytes 2359296 | tf_op jit(solution)/shard_map/convert_element_type | solution.py:1039
  185.3 0.0 copy-start
  185.3 1.3 reshape.69
  186.7 0.0 copy-start.4
  186.7 0.0 copy-start.2
  186.7 0.2 copy.22
  186.8 0.0 copy-start.1
  186.8 1.1 reshape.70
  187.9 0.0 copy-done.3
  187.9 0.1 copy.27
  188.0 1.9 fusion
  189.9 0.7 dynamic-slice_reduce_fusion
  190.6 0.0 copy-done
  190.6 0.9 copy.35
  191.5 0.0 copy-done.4
  191.5 0.7 copy.36
  192.1 0.0 copy-done.2
  192.1 0.8 copy.37
  193.0 0.0 copy-done.1
  193.0 0.8 copy.38
  (4 shorter events, 0.0 us)
Async XLA Ops:
  182.9 5.0 %copy-start.3 = (f32[16,48,128]{2,1,0:T(8,128)S(1)}, f32[16,48,128]{2,1,0:T(8,128)}, u32[]{:S(2)}) copy-start(f32[16,48,128]{2,1,0:T(8,128)} %get-tuple-element.21) | copy-start | bytes 1179652
  185.3 5.3 %copy-start = (bf16[1,512,768]{2,1,0:T(8,128)(2,1)S(1)}, bf16[1,512,768]{2,1,0:T(8,128)(2,1)}, u32[]{:S(2)}) copy-start(bf16[1,512,768]{2,1,0:T(8,128)(2,1)} %get-tuple-element.41) | copy-start | bytes 2359300
  186.7 4.8 %copy-start.4 = (f32[48,768]{1,0:T(8,128)S(1)}, f32[48,768]{1,0:T(8,128)}, u32[]{:S(2)}) copy-start(f32[48,768]{1,0:T(8,128)} %get-tuple-element.44) | copy-start | bytes 442372
  186.7 5.5 %copy-start.2 = (f32[48,3072]{1,0:T(8,128)S(1)}, f32[48,3072]{1,0:T(8,128)}, u32[]{:S(2)}) copy-start(f32[48,3072]{1,0:T(8,128)} %get-tuple-element.45) | copy-start | bytes 1769476
  186.8 6.1 %copy-start.1 = (f32[192,768]{1,0:T(8,128)S(1)}, f32[192,768]{1,0:T(8,128)}, u32[]{:S(2)}) copy-start(f32[192,768]{1,0:T(8,128)} %get-tuple-element.46) | copy-start | bytes 1769476
